TPU v7x, 32 devices: a whole 2x2x4 slice. The times are simulated.
32 devices in a mesh: groups: 2 (over y), dp: 4 (over z), expert: 2 (over x), tensor: 2 (over core).
Axes of the slice: x: 2, y: 2, z: 4, core: 2. Of those that a mesh axis runs over, the one named last changes fastest.
Arguments:
- tokens: bfloat16 [2048, 6144], P(('groups', 'dp', 'expert'), 'tensor'), parts along dimension 0, may hold values from -6 to 6
- routes: int32 [2048, 2], P(('groups', 'dp', 'expert')), parts along dimension 0, may hold values from 0 to 3, all different within a row; in each aligned block of 128 rows (0 to 127, 128 to 255, ...) at most 80 rows name the same one
- route_weight: float32 [2048, 2], P(('groups', 'dp', 'expert')), parts along dimension 0, may hold values from 0.2 to 1
- block_tenant: int32 [16], P('groups'), parts along dimension 0, may hold values from 0 to 31
- page_table: int32 [4, 32], replicated, may hold values from 0 to 31, each once within a row
- adapter_in: bfloat16 [4, 32, 32, 6144], P('expert', None, None, ('tensor', 'dp')), may hold values from -0.078125 to 0.078125
- adapter_down: bfloat16 [4, 32, 16, 6144], P('expert', None, None, ('tensor', 'dp')), may hold values from -1.5 to 1.5
- upstream: bfloat16 [2048, 6144], P(('groups', 'dp', 'expert'), 'tensor'), parts along dimension 0, may hold values from -6 to 6
Outputs:
- adapted: bfloat16 [2048, 6144], P(('groups', 'dp', 'expert'), 'tensor'), parts along dimension 0
- grad_tokens: bfloat16 [2048, 6144], P(('groups', 'dp', 'expert'), 'tensor'), parts along dimension 0
- grad_weight: float32 [2048, 2], P(('groups', 'dp', 'expert')), parts along dimension 0
- grad_in: float32 [8, 32, 32, 6144], P(('groups', 'expert'), None, None, ('tensor', 'dp')), parts along dimension 0
- grad_down: float32 [8, 32, 16, 6144], P(('groups', 'expert'), None, None, ('tensor', 'dp')), parts along dimension 0
There are 2 independent parts, one for each index of `groups`. A program takes and returns all parts, laid end to end along the dimension named above; an argument that names none is the same for every part. Nothing has to cross between parts.
Inputs may be any that keep to these rules, and one draw needn't show every extreme that they name: `routes`: the two experts of a token differ; among the 128 tokens of one device no expert is named more than 80 times, and some device names some expert exactly 80 times.
All inputs are finite; a program needn't handle non-finite values.
Results may differ from a plain program's by a relative error of at most 0.0065.
Values may be sent and summed in bfloat16 or wider, within the bound.
A program may use at most 128 MiB of HBM per device.

v0:
```python
import functools

import jax
import jax.numpy as jnp
from jax import lax
from jax.experimental import pallas as pl
from jax.experimental.pallas import tpu as pltpu
from jax.sharding import PartitionSpec as P

BF16 = jnp.bfloat16
F32 = jnp.float32
MESH = pl.DeviceIdType.MESH
LAST_LAST = (((1,), (1,)), ((), ()))
PLAIN = (((1,), (0,)), ((), ()))


def matmul(left, right, dims=PLAIN):
    return lax.dot_general(left, right, dims, preferred_element_type=F32)


def step_order(size):
    return sorted(range(size), key=lambda step: -min(step, size - step))


def adapter_kernel(
    sizes,
    block_tenant, page_table, routes, weights, tokens, upstream, adapter_in, adapter_down,
    adapted, grad_tokens, grad_weight, grad_parts,
    tenants, table, route, weight_of,
    all_in, all_down, tok, cot, pages_out, pages, sums_out, sums_in, proj_out, proj_in,
    parts_out, adapted_v, grad_tokens_v, grad_weight_v,
    small_sem, load_sem, token_sem, page_send, page_recv, swap_send, swap_recv,
    part_send, part_recv, own_sem, out_sem,
):
    dp_size, ex_size, exp_dev, rank, piece, tok_dev, top = sizes
    wide = ex_size * exp_dev * rank
    kinds = (pl.ds(0, 2), pl.ds(2, 1))
    me_dp = lax.axis_index("dp")
    me_ex = lax.axis_index("expert")
    other_core = lax.rem(lax.axis_index("tensor") + 1, 2)
    dp_order = step_order(dp_size)
    peers = [(dz, dx) for dz in dp_order for dx in range(ex_size) if (dz, dx) != (0, 0)]

    def dp_at(dz):
        return lax.rem(me_dp + dz, dp_size)

    def ex_at(dx):
        return lax.rem(me_ex + dx, ex_size)

    def columns(p):
        return pl.ds(p * piece, piece)

    barrier = pltpu.get_barrier_semaphore()
    for dz, dx in peers:
        pl.semaphore_signal(
            barrier, inc=1, device_id={"dp": dp_at(dz), "expert": ex_at(dx)}, device_id_type=MESH
        )
    pl.semaphore_signal(barrier, inc=1, device_id={"tensor": other_core}, device_id_type=MESH)

    small_loads = [
        pltpu.make_async_copy(source, target, small_sem.at[i])
        for i, (source, target) in enumerate(
            [(block_tenant, tenants), (page_table, table), (routes, route), (weights, weight_of)]
        )
    ]
    load_in = pltpu.make_async_copy(adapter_in, all_in, load_sem.at[0])
    load_down = pltpu.make_async_copy(adapter_down, all_down, load_sem.at[1])
    tok_loads = [
        pltpu.make_async_copy(tokens.at[:, columns(p)], tok.at[p], token_sem.at[0, p])
        for p in range(dp_size)
    ]
    cot_loads = [
        pltpu.make_async_copy(upstream.at[:, columns(p)], cot.at[p], token_sem.at[1, p])
        for p in range(dp_size)
    ]
    for load in small_loads + [load_in, load_down] + tok_loads + cot_loads:
        load.start()

    def page_copy(i, dz, dx, place):
        return pltpu.make_async_remote_copy(
            src_ref=pages_out.at[dp_at(dz), ex_at(dx), kinds[i]],
            dst_ref=pages.at[place[0], kinds[i], place[1]],
            send_sem=page_send.at[i, dz, dx],
            recv_sem=page_recv.at[i, place[0], place[1]],
            device_id={"dp": dp_at(dz), "expert": ex_at(dx)},
            device_id_type=MESH,
        )

    def part_copy(i, dz, dx, place):
        return pltpu.make_async_remote_copy(
            src_ref=parts_out.at[dp_at(dz), kinds[i], ex_at(dx)],
            dst_ref=grad_parts.at[place[0], place[1], kinds[i]],
            send_sem=part_send.at[i, dz, dx],
            recv_sem=part_recv.at[i, place[0], place[1]],
            device_id={"dp": dp_at(dz), "expert": ex_at(dx)},
            device_id_type=MESH,
        )

    def swap_copy(i, out_ref, in_ref):
        return pltpu.make_async_remote_copy(
            src_ref=out_ref,
            dst_ref=in_ref,
            send_sem=swap_send.at[i],
            recv_sem=swap_recv.at[i],
            device_id={"tensor": other_core},
            device_id_type=MESH,
        )

    def send_pages(i):
        for dz, dx in peers + [(0, 0)]:
            tenant = tenants[dp_at(dz) * ex_size + ex_at(dx)]
            for local in range(exp_dev):
                slot = table[me_ex * exp_dev + local, tenant]
                if i == 0:
                    page = all_in[local, slot]
                    rows = {0: page[:rank], 1: page[rank:]}
                else:
                    rows = {2: all_down[local, slot]}
                for kind, value in rows.items():
                    if (dz, dx) == (0, 0):
                        pages[me_dp, kind, me_ex, local] = value
                    else:
                        pages_out[dp_at(dz), ex_at(dx), kind, local] = value
            if (dz, dx) != (0, 0):
                page_copy(i, dz, dx, (me_dp, me_ex)).start()

    def project(i, rows):
        total = None
        for dz in [0] + dp_order[:-1]:
            d = dp_at(dz)
            for dx in range(ex_size):
                if (dz, dx) != (0, 0):
                    page_copy(i, dz, dx, (d, ex_at(dx))).wait_recv()
            page = pages[d, 0:2] if i == 0 else pages[d, 2]
            part = matmul(page.reshape(-1, piece), rows[d], LAST_LAST)
            total = part if total is None else total + part
        return total

    def send_parts(i, values, rows):
        for dz in dp_order:
            d = dp_at(dz)
            part = matmul(values, rows[d]).astype(BF16)
            if i == 0:
                parts_out[d, 0:2] = part.reshape(2, ex_size, exp_dev, rank, piece)
            else:
                parts_out[d, 2] = part.reshape(ex_size, exp_dev, rank, piece)
            for dx in range(ex_size):
                if (dz, dx) != (0, 0):
                    part_copy(i, dz, dx, (me_dp, me_ex)).start()

    small_loads[0].wait()
    small_loads[1].wait()
    load_in.wait()
    pl.semaphore_wait(barrier, len(peers) + 1)
    send_pages(0)
    load_down.wait()
    send_pages(1)

    for load in small_loads[2:] + tok_loads:
        load.wait()
    expert_of = lax.broadcasted_iota(jnp.int32, (wide, tok_dev), 0) // rank
    chosen = [route[k : k + 1, :] == expert_of for k in range(top)]
    weight = sum(jnp.where(chosen[k], weight_of[k : k + 1, :], 0.0) for k in range(top))
    pre = project(0, tok)
    sums_out[...] = pre
    swap_pre = swap_copy(0, sums_out, sums_in)
    swap_pre.start()
    for load in cot_loads:
        load.wait()
    swap_pre.wait_recv()
    pre = pre + sums_in[...]
    gate = pre[:wide]
    upv = pre[wide:]
    sig = jax.nn.sigmoid(gate)
    act = gate * sig
    hidden = (act * upv).astype(BF16).astype(F32)
    weighted = weight * hidden
    send_parts(1, weighted.astype(BF16), cot)

    proj = project(1, cot)
    proj_out[...] = proj
    swap_proj = swap_copy(1, proj_out, proj_in)
    swap_proj.start()
    swap_proj.wait_recv()
    proj = proj + proj_in[...]
    hgrad = weight * proj
    lowrank = jnp.concatenate(
        [hgrad * upv * sig * (1.0 + gate * (1.0 - sig)), hgrad * act], axis=0
    )
    send_parts(0, lowrank.astype(BF16), tok)
    own = pltpu.make_async_copy(
        parts_out.at[me_dp, :, me_ex], grad_parts.at[me_dp, me_ex], own_sem
    )
    own.start()

    weighted = weighted.T.astype(BF16)
    lowrank = lowrank.T.astype(BF16)
    outs = []
    for p in range(dp_size):
        adapted_v[p] = matmul(weighted, pages[p, 2].reshape(wide, piece)).astype(BF16)
        outs.append(
            pltpu.make_async_copy(adapted_v.at[p], adapted.at[:, columns(p)], out_sem.at[0, p])
        )
        outs[-1].start()
        grad_tokens_v[p] = matmul(lowrank, pages[p, 0:2].reshape(2 * wide, piece)).astype(BF16)
        outs.append(
            pltpu.make_async_copy(
                grad_tokens_v.at[p], grad_tokens.at[:, columns(p)], out_sem.at[1, p]
            )
        )
        outs[-1].start()
    product = hidden * proj
    for k in range(top):
        grad_weight_v[k : k + 1, :] = jnp.sum(
            jnp.where(chosen[k], product, 0.0), axis=0, keepdims=True
        )
    outs.append(pltpu.make_async_copy(grad_weight_v, grad_weight, out_sem.at[2, 0]))
    outs[-1].start()

    for out in outs:
        out.wait()
    swap_pre.wait_send()
    swap_proj.wait_send()
    own.wait()
    for i in range(2):
        for dz, dx in peers:
            page_copy(i, dz, dx, (me_dp, me_ex)).wait_send()
    for i in (1, 0):
        for dz, dx in peers:
            part_copy(i, dz, dx, (me_dp, me_ex)).wait_send()
            part_copy(i, dz, dx, (dp_at(dz), ex_at(dx))).wait_recv()


def scatter_kernel(
    sizes, slots,
    block_tenant, page_table, parts, adapted, grad_tokens,
    grad_in, grad_down, adapted_out, grad_tokens_out,
    tenants, table, parts_v, small_sem, parts_sem, pass_sem,
):
    dp_size, ex_size, exp_dev, rank = sizes
    local = pl.program_id(0)
    chunk = pl.program_id(1)
    loads = [
        pltpu.make_async_copy(block_tenant, tenants, small_sem.at[0]),
        pltpu.make_async_copy(page_table, table, small_sem.at[1]),
        pltpu.make_async_copy(parts, parts_v, parts_sem),
    ]
    passed = [
        pltpu.make_async_copy(adapted, adapted_out, pass_sem.at[0]),
        pltpu.make_async_copy(grad_tokens, grad_tokens_out, pass_sem.at[1]),
    ]
    first = (local == 0) & (chunk == 0)

    @pl.when(first)
    def _():
        for load in loads + passed:
            load.start()

    grad_in[...] = jnp.zeros_like(grad_in)
    grad_down[...] = jnp.zeros_like(grad_down)

    @pl.when(first)
    def _():
        for load in loads:
            load.wait()

    expert = lax.axis_index("expert") * exp_dev + local
    for d in range(dp_size):
        for x in range(ex_size):
            place = table[expert, tenants[d * ex_size + x]] - chunk * slots

            @pl.when((place >= 0) & (place < slots))
            def _():
                grad_in[0, place, :rank] += parts_v[d, x, 0, local].astype(F32)
                grad_in[0, place, rank:] += parts_v[d, x, 1, local].astype(F32)
                grad_down[0, place] += parts_v[d, x, 2, local].astype(F32)

    @pl.when((local == pl.num_programs(0) - 1) & (chunk == pl.num_programs(1) - 1))
    def _():
        for copy in passed:
            copy.wait()


def paged(
    tokens, routes, route_weight, block_tenant, page_table, adapter_in, adapter_down, upstream
):
    tok_dev, half = tokens.shape
    top = routes.shape[1]
    exp_dev, tenants, _, piece = adapter_in.shape
    rank = adapter_down.shape[2]
    dp_size = lax.axis_size("dp")
    ex_size = lax.axis_size("expert")
    wide = ex_size * exp_dev * rank
    sizes = (dp_size, ex_size, exp_dev, rank, piece, tok_dev, top)
    any_spec = pl.BlockSpec(memory_space=pl.ANY)
    dma = pltpu.SemaphoreType.DMA
    parts_shape = (dp_size, ex_size, 3, exp_dev, rank, piece)
    rows_shape = jax.ShapeDtypeStruct((tok_dev, half), BF16)
    small_scratch = [
        pltpu.SMEM(block_tenant.shape, jnp.int32),
        pltpu.SMEM(page_table.shape, jnp.int32),
    ]
    adapted, grad_tokens, grad_weight, parts = pl.pallas_call(
        functools.partial(adapter_kernel, sizes),
        out_shape=(
            rows_shape,
            rows_shape,
            jax.ShapeDtypeStruct((top, tok_dev), F32),
            jax.ShapeDtypeStruct(parts_shape, BF16),
        ),
        in_specs=[any_spec] * 8,
        out_specs=(any_spec,) * 4,
        scratch_shapes=small_scratch
        + [
            pltpu.VMEM((top, tok_dev), jnp.int32),
            pltpu.VMEM((top, tok_dev), F32),
            pltpu.VMEM(adapter_in.shape, BF16),
            pltpu.VMEM(adapter_down.shape, BF16),
            pltpu.VMEM((dp_size, tok_dev, piece), BF16),
            pltpu.VMEM((dp_size, tok_dev, piece), BF16),
            pltpu.VMEM(parts_shape, BF16),
            pltpu.VMEM((dp_size, 3, ex_size, exp_dev, rank, piece), BF16),
            pltpu.VMEM((2 * wide, tok_dev), F32),
            pltpu.VMEM((2 * wide, tok_dev), F32),
            pltpu.VMEM((wide, tok_dev), F32),
            pltpu.VMEM((wide, tok_dev), F32),
            pltpu.VMEM((dp_size, 3, ex_size, exp_dev, rank, piece), BF16),
            pltpu.VMEM((dp_size, tok_dev, piece), BF16),
            pltpu.VMEM((dp_size, tok_dev, piece), BF16),
            pltpu.VMEM((top, tok_dev), F32),
            dma((4,)),
            dma((2,)),
            dma((2, dp_size)),
            dma((2, dp_size, ex_size)),
            dma((2, dp_size, ex_size)),
            dma((2,)),
            dma((2,)),
            dma((2, dp_size, ex_size)),
            dma((2, dp_size, ex_size)),
            dma,
            dma((3, dp_size)),
        ],
        compiler_params=pltpu.CompilerParams(
            collective_id=0, has_side_effects=True, vmem_limit_bytes=60 << 20
        ),
    )(
        block_tenant, page_table, routes.T, route_weight.T,
        tokens, upstream, adapter_in, adapter_down,
    )
    slots = 8
    grad_in, grad_down, adapted, grad_tokens = pl.pallas_call(
        functools.partial(scatter_kernel, (dp_size, ex_size, exp_dev, rank), slots),
        grid=(exp_dev, tenants // slots),
        out_shape=(
            jax.ShapeDtypeStruct((exp_dev, tenants, 2 * rank, piece), F32),
            jax.ShapeDtypeStruct((exp_dev, tenants, rank, piece), F32),
            rows_shape,
            rows_shape,
        ),
        in_specs=[any_spec] * 5,
        out_specs=(
            pl.BlockSpec((1, slots, 2 * rank, piece), lambda i, j: (i, j, 0, 0)),
            pl.BlockSpec((1, slots, rank, piece), lambda i, j: (i, j, 0, 0)),
            any_spec,
            any_spec,
        ),
        scratch_shapes=small_scratch
        + [pltpu.VMEM(parts_shape, BF16), dma((2,)), dma, dma((2,))],
        compiler_params=pltpu.CompilerParams(vmem_limit_bytes=60 << 20),
    )(block_tenant, page_table, parts, adapted, grad_tokens)
    return (adapted, grad_tokens, grad_weight.T, grad_in, grad_down)


def feature_sum(partial_value):
    return lax.psum(partial_value, "tensor")


def swap_blocks(block):
    return lax.all_to_all(block, "expert", split_axis=0, concat_axis=0, tiled=True)


def routed(
    tokens, routes, route_weight, block_tenant, page_table, adapter_in, adapter_down, upstream
):
    tok_dev, half = tokens.shape
    top = routes.shape[1]
    exp_dev = adapter_in.shape[0]
    tenants = adapter_in.shape[1]
    rank = adapter_down.shape[2]
    piece = adapter_in.shape[3]
    dp_size = lax.axis_size("dp")
    ex_size = lax.axis_size("expert")
    experts = exp_dev * ex_size
    column = lax.axis_index("expert")
    tenant_grid = block_tenant.reshape(dp_size, ex_size)
    local_table = lax.dynamic_slice_in_dim(page_table, column * exp_dev, exp_dev, 0)
    wanted = local_table[:, tenant_grid]
    flat_in = adapter_in.reshape(exp_dev, tenants, 2 * rank * piece)
    flat_down = adapter_down.reshape(exp_dev, tenants, rank * piece)
    send_in = jnp.stack([flat_in[local][wanted[local]] for local in range(exp_dev)], axis=1)
    send_down = jnp.stack([flat_down[local][wanted[local]] for local in range(exp_dev)], axis=1)
    got_in, got_down = (
        lax.all_to_all(send_in, "dp", split_axis=0, concat_axis=0, tiled=True),
        lax.all_to_all(send_down, "dp", split_axis=0, concat_axis=0, tiled=True),
    )
    page_in = (
        got_in.reshape(dp_size, exp_dev, ex_size, 2 * rank, piece)
        .transpose(1, 2, 3, 0, 4)
        .reshape(exp_dev, ex_size, 2 * rank, half)
    )
    page_down = (
        got_down.reshape(dp_size, exp_dev, ex_size, rank, piece)
        .transpose(1, 2, 3, 0, 4)
        .reshape(exp_dev, ex_size, rank, half)
    )
    scaled = (route_weight[:, :, None] * upstream[:, None, :].astype(jnp.float32)).astype(
        jnp.bfloat16
    )
    cap = 5 * tok_dev * top // (4 * experts)
    slot_count = experts * cap
    flat_routes = routes.reshape(-1)
    hits = (flat_routes[:, None] == jnp.arange(experts, dtype=jnp.int32)[None, :]).astype(jnp.int32)
    position = jnp.sum((jnp.cumsum(hits, axis=0) - 1) * hits, axis=1)
    slot = flat_routes * cap + position
    placing = (slot[None, :] == jnp.arange(slot_count, dtype=jnp.int32)[:, None]).astype(
        jnp.bfloat16
    )
    placing_tok = jnp.sum(placing.reshape(slot_count, tok_dev, top), axis=2)
    rows_send = jnp.dot(placing_tok, tokens, preferred_element_type=jnp.float32).astype(
        jnp.bfloat16
    )
    arrived = swap_blocks(rows_send).reshape(ex_size, exp_dev, cap, half)
    pre = feature_sum(
        jnp.einsum("kecd,ekrd->kecr", arrived, page_in, preferred_element_type=jnp.float32)
    )
    gate = pre[..., :rank]
    upv = pre[..., rank:]
    sig = jax.nn.sigmoid(gate)
    act = gate * sig
    hidden = (act * upv).astype(jnp.bfloat16)
    branch = jnp.einsum(
        "kecr,ekrd->kecd", hidden, page_down, preferred_element_type=jnp.float32
    ).astype(jnp.bfloat16)
    returned = swap_blocks(branch.reshape(slot_count, half))
    picked = returned[slot].reshape(tok_dev, top, half)
    adapted = jnp.sum(route_weight[:, :, None] * picked.astype(jnp.float32), axis=1).astype(
        jnp.bfloat16
    )
    grad_weight = feature_sum(
        jnp.einsum("td,tkd->tk", upstream, picked, preferred_element_type=jnp.float32)
    )
    cot_send = jnp.dot(
        placing, scaled.reshape(tok_dev * top, half), preferred_element_type=jnp.float32
    ).astype(jnp.bfloat16)
    cot_blocks = swap_blocks(cot_send).reshape(ex_size, exp_dev, cap, half)
    hgrad = feature_sum(
        jnp.einsum("kecd,ekrd->kecr", cot_blocks, page_down, preferred_element_type=jnp.float32)
    )
    lowrank = jnp.concatenate(
        [hgrad * upv * sig * (1.0 + gate * (1.0 - sig)), hgrad * act], axis=3
    ).astype(jnp.bfloat16)
    input_grad = jnp.einsum(
        "kecr,ekrd->kecd", lowrank, page_in, preferred_element_type=jnp.float32
    ).astype(jnp.bfloat16)
    req_in = jnp.einsum("kecr,kecd->ekrd", lowrank, arrived, preferred_element_type=jnp.float32)
    req_down = jnp.einsum("kecr,kecd->ekrd", hidden, cot_blocks, preferred_element_type=jnp.float32)
    grad_back = swap_blocks(input_grad.reshape(slot_count, half))
    grad_tokens = jnp.sum(
        grad_back[slot].reshape(tok_dev, top, half).astype(jnp.float32), axis=1
    ).astype(jnp.bfloat16)
    out_in = (
        req_in.reshape(exp_dev, ex_size, 2 * rank, dp_size, piece)
        .transpose(3, 0, 1, 2, 4)
        .reshape(dp_size, exp_dev, ex_size, 2 * rank * piece)
    )
    out_down = (
        req_down.reshape(exp_dev, ex_size, rank, dp_size, piece)
        .transpose(3, 0, 1, 2, 4)
        .reshape(dp_size, exp_dev, ex_size, rank * piece)
    )
    recv_in, recv_down = (
        lax.all_to_all(out_in, "dp", split_axis=0, concat_axis=0, tiled=True),
        lax.all_to_all(out_down, "dp", split_axis=0, concat_axis=0, tiled=True),
    )
    sums_in = []
    sums_down = []
    for local in range(exp_dev):
        owners = wanted[local].reshape(-1)
        sums_in.append(
            jnp.zeros((tenants, 2 * rank * piece), jnp.float32)
            .at[owners]
            .add(recv_in[:, local].reshape(dp_size * ex_size, -1))
        )
        sums_down.append(
            jnp.zeros((tenants, rank * piece), jnp.float32)
            .at[owners]
            .add(recv_down[:, local].reshape(dp_size * ex_size, -1))
        )
    grad_in = jnp.stack(sums_in, axis=0).reshape(exp_dev, tenants, 2 * rank, piece)
    grad_down = jnp.stack(sums_down, axis=0).reshape(exp_dev, tenants, rank, piece)
    return (adapted, grad_tokens, grad_weight, grad_in, grad_down)


def shards(*arrays):
    rank, piece = arrays[6].shape[2:]
    whole_tiles = piece % 128 == 0 and rank % 16 == 0 and lax.axis_size("tensor") == 2
    return paged(*arrays) if whole_tiles else routed(*arrays)


def solution(mesh):
    return jax.shard_map(
        shards,
        mesh=mesh,
        in_specs=(
            P(("groups", "dp", "expert"), "tensor"),
            P(("groups", "dp", "expert"), None),
            P(("groups", "dp", "expert"), None),
            P("groups"),
            P(),
            P("expert", None, None, ("tensor", "dp")),
            P("expert", None, None, ("tensor", "dp")),
            P(("groups", "dp", "expert"), "tensor"),
        ),
        out_specs=(
            P(("groups", "dp", "expert"), "tensor"),
            P(("groups", "dp", "expert"), "tensor"),
            P(("groups", "dp", "expert"), None),
            P(("groups", "expert"), None, None, ("tensor", "dp")),
            P(("groups", "expert"), None, None, ("tensor", "dp")),
        ),
        check_vma=False,
    )
```

profile of v0, /device:TPU:17, one launch (start us, length us, event | category | flops | bytes accessed | tf_op | source)
XLA Modules:
  0.0 108.4 jit_solution(3308803497201080255)
XLA Ops:
  0.6 56.6 %shard_map.119 = (bf16[128,3072]{1,0:T(8,128)(2,1)}, bf16[128,3072]{1,0:T(8,128)(2,1)}, f32[2,128]{1,0:T(2,128)}, bf16[4,2,3,2,16,768]{5,4,3,2,1,0:T(8,128)(2,1)}) custom-call(s32[8]{0:T(128)} %block_tenant.3, s32[4,32]{1,0:T(4,128)} %page_table.3, s32[2,128]{1,0:T(2,128)} %bitcast.4, f32[2,128]{1,0:T(2,128)} %bitcast.5, bf16[128,3072]{1,0:T(8,128)(2,1)} %tokens.1, ...), custom_call_target="tpu_custom_call" | custom-call | tf_op jit(solution)/shard_map/pallas_call | solution.py:303
  57.3 49.8 %shard_map.120 = (f32[2,32,32,768]{3,2,1,0:T(8,128)}, f32[2,32,16,768]{3,2,1,0:T(8,128)}, bf16[128,3072]{1,0:T(8,128)(2,1)}, bf16[128,3072]{1,0:T(8,128)(2,1)}) custom-call(s32[8]{0:T(128)} %block_tenant.3, s32[4,32]{1,0:T(4,128)} %page_table.3, bf16[4,2,3,2,16,768]{5,4,3,2,1,0:T(8,128)(2,1)} %get-tuple-element.13.parts, ...), custom_call_target="tpu_custom_call" | custom-call | tf_op jit(solution)/shard_map/pallas_call | solution.py:351
  107.1 1.2 %copy.14 = f32[128,2]{0,1:T(2,128)} copy(f32[128,2]{0,1:T(2,128)} %bitcast.3) | data formatting | bytes 2048
where the time goes:
time: 109 us; the launch traced here: 108 us
  Pallas kernels  106 us (97%)
  local copies, waits for them, and re-layouts  1.25 us (1%)
    pallas_call x1, Pallas kernels, paged(): pl.pallas_call(functools.partial(adapter_kernel, sizes), out_shape=(rows_...  56.6 us
    pallas_call x1, Pallas kernels, paged(): pl.pallas_call(functools.partial(scatter_kernel, (dp_size, ex_size, exp_d...  49.8 us

commit v1 on v0

--- a/solution.py
+++ b/solution.py
@@ -233,9 +233,10 @@
 
 def scatter_kernel(
     sizes, slots,
-    block_tenant, page_table, parts, adapted, grad_tokens,
-    grad_in, grad_down, adapted_out, grad_tokens_out,
-    tenants, table, parts_v, small_sem, parts_sem, pass_sem,
+    block_tenant, page_table, parts, adapted, grad_tokens, grad_weight,
+    grad_in, grad_down, adapted_out, grad_tokens_out, grad_weight_out,
+    tenants, table, parts_v, adapted_v, grad_tokens_v, grad_weight_v,
+    small_sem, parts_sem, enter_sem, leave_sem,
 ):
     dp_size, ex_size, exp_dev, rank = sizes
     local = pl.program_id(0)
@@ -246,23 +247,39 @@
         pltpu.make_async_copy(parts, parts_v, parts_sem),
     ]
     passed = [
-        pltpu.make_async_copy(adapted, adapted_out, pass_sem.at[0]),
-        pltpu.make_async_copy(grad_tokens, grad_tokens_out, pass_sem.at[1]),
-    ]
-    first = (local == 0) & (chunk == 0)
-
-    @pl.when(first)
+        (adapted, adapted_v, adapted_out),
+        (grad_tokens, grad_tokens_v, grad_tokens_out),
+        (grad_weight, grad_weight_v, grad_weight_out),
+    ]
+    enter = [
+        pltpu.make_async_copy(source, held, enter_sem.at[i])
+        for i, (source, held, _) in enumerate(passed)
+    ]
+    leave = [
+        pltpu.make_async_copy(held, target, leave_sem.at[i])
+        for i, (_, held, target) in enumerate(passed)
+    ]
+    step = local * pl.num_programs(1) + chunk
+
+    @pl.when(step == 0)
     def _():
-        for load in loads + passed:
+        for load in loads + enter:
             load.start()
 
     grad_in[...] = jnp.zeros_like(grad_in)
     grad_down[...] = jnp.zeros_like(grad_down)
 
-    @pl.when(first)
+    @pl.when(step == 0)
     def _():
         for load in loads:
             load.wait()
+
+    @pl.when(step == 1)
+    def _():
+        for load in enter:
+            load.wait()
+        for store in leave:
+            store.start()
 
     expert = lax.axis_index("expert") * exp_dev + local
     for d in range(dp_size):
@@ -275,10 +292,10 @@
                 grad_in[0, place, rank:] += parts_v[d, x, 1, local].astype(F32)
                 grad_down[0, place] += parts_v[d, x, 2, local].astype(F32)
 
-    @pl.when((local == pl.num_programs(0) - 1) & (chunk == pl.num_programs(1) - 1))
+    @pl.when(step == pl.num_programs(0) * pl.num_programs(1) - 1)
     def _():
-        for copy in passed:
-            copy.wait()
+        for store in leave:
+            store.wait()
 
 
 def paged(
@@ -295,6 +312,7 @@
     any_spec = pl.BlockSpec(memory_space=pl.ANY)
     dma = pltpu.SemaphoreType.DMA
     parts_shape = (dp_size, ex_size, 3, exp_dev, rank, piece)
+    weight_shape = jax.ShapeDtypeStruct((top, tok_dev), F32)
     rows_shape = jax.ShapeDtypeStruct((tok_dev, half), BF16)
     small_scratch = [
         pltpu.SMEM(block_tenant.shape, jnp.int32),
@@ -305,7 +323,7 @@
         out_shape=(
             rows_shape,
             rows_shape,
-            jax.ShapeDtypeStruct((top, tok_dev), F32),
+            weight_shape,
             jax.ShapeDtypeStruct(parts_shape, BF16),
         ),
         in_specs=[any_spec] * 8,
@@ -348,7 +366,7 @@
         tokens, upstream, adapter_in, adapter_down,
     )
     slots = 8
-    grad_in, grad_down, adapted, grad_tokens = pl.pallas_call(
+    grad_in, grad_down, adapted, grad_tokens, grad_weight = pl.pallas_call(
         functools.partial(scatter_kernel, (dp_size, ex_size, exp_dev, rank), slots),
         grid=(exp_dev, tenants // slots),
         out_shape=(
@@ -356,18 +374,29 @@
             jax.ShapeDtypeStruct((exp_dev, tenants, rank, piece), F32),
             rows_shape,
             rows_shape,
+            weight_shape,
         ),
-        in_specs=[any_spec] * 5,
+        in_specs=[any_spec] * 6,
         out_specs=(
             pl.BlockSpec((1, slots, 2 * rank, piece), lambda i, j: (i, j, 0, 0)),
             pl.BlockSpec((1, slots, rank, piece), lambda i, j: (i, j, 0, 0)),
             any_spec,
             any_spec,
+            any_spec,
         ),
         scratch_shapes=small_scratch
-        + [pltpu.VMEM(parts_shape, BF16), dma((2,)), dma, dma((2,))],
+        + [
+            pltpu.VMEM(parts_shape, BF16),
+            pltpu.VMEM((tok_dev, half), BF16),
+            pltpu.VMEM((tok_dev, half), BF16),
+            pltpu.VMEM((top, tok_dev), F32),
+            dma((2,)),
+            dma,
+            dma((3,)),
+            dma((3,)),
+        ],
         compiler_params=pltpu.CompilerParams(vmem_limit_bytes=60 << 20),
-    )(block_tenant, page_table, parts, adapted, grad_tokens)
+    )(block_tenant, page_table, parts, adapted, grad_tokens, grad_weight)
     return (adapted, grad_tokens, grad_weight.T, grad_in, grad_down)
 
 

time: 109 us -> 65.7 us (0.60)
  Pallas kernels: 106 us -> 64.2 us
  local copies, waits for them, and re-layouts: 1.25 us -> 0 us
    pallas_call x1, Pallas kernels: 49.8 us -> 7.54 us  [paged(): pl.pallas_call(functools.partial(scatter_kernel, (dp_size, ex_size, exp_d...]
    unnamed x1 -> x0, local copies, waits for them, and re-layouts: 1.25 us -> none
where the time goes in v1:
time: 65.7 us; the launch traced here: 64.8 us
  Pallas kernels  64.2 us (98%)
    pallas_call x1, Pallas kernels, paged(): pl.pallas_call(functools.partial(adapter_kernel, sizes), out_shape=(rows_...  56.6 us
    pallas_call x1, Pallas kernels, paged(): pl.pallas_call(functools.partial(scatter_kernel, (dp_size, ex_size, exp_d...  7.54 us

profile of v1, /device:TPU:17, one launch (start us, length us, event | category | flops | bytes accessed | tf_op | source)
XLA Modules:
  0.0 64.8 jit_solution(17849511932893412655)
XLA Ops:
  0.6 56.6 %shard_map.119 = (bf16[128,3072]{1,0:T(8,128)(2,1)}, bf16[128,3072]{1,0:T(8,128)(2,1)}, f32[2,128]{1,0:T(2,128)}, bf16[4,2,3,2,16,768]{5,4,3,2,1,0:T(8,128)(2,1)}) custom-call(s32[8]{0:T(128)} %block_tenant.3, s32[4,32]{1,0:T(4,128)} %page_table.3, s32[2,128]{1,0:T(2,128)} %bitcast.3, f32[2,128]{1,0:T(2,128)} %bitcast.4, bf16[128,3072]{1,0:T(8,128)(2,1)} %tokens.1, ...), custom_call_target="tpu_custom_call" | custom-call | tf_op jit(solution)/shard_map/pallas_call | solution.py:321
  57.3 7.5 %shard_map.120 = (f32[2,32,32,768]{3,2,1,0:T(8,128)}, f32[2,32,16,768]{3,2,1,0:T(8,128)}, bf16[128,3072]{1,0:T(8,128)(2,1)}, bf16[128,3072]{1,0:T(8,128)(2,1)}, f32[2,128]{1,0:T(2,128)}) custom-call(s32[8]{0:T(128)} %block_tenant.3, s32[4,32]{1,0:T(4,128)} %page_table.3, bf16[4,2,3,2,16,768]{5,4,3,2,1,0:T(8,128)(2,1)} %get-tuple-element.14.parts, ...), custom_call_target="tpu_custom_call" | custom-call | tf_op jit(solution)/shard_map/pallas_call | solution.py:369

commit v2 on v1

--- a/solution.py
+++ b/solution.py
@@ -19,7 +19,8 @@
 
 
 def step_order(size):
-    return sorted(range(size), key=lambda step: -min(step, size - step))
+    half = size // 2
+    return list(range(half, size)) + list(range(1, half)) + [0]
 
 
 def adapter_kernel(
@@ -39,10 +40,12 @@
     me_ex = lax.axis_index("expert")
     other_core = lax.rem(lax.axis_index("tensor") + 1, 2)
     dp_order = step_order(dp_size)
-    peers = [(dz, dx) for dz in dp_order for dx in range(ex_size) if (dz, dx) != (0, 0)]
+    peers = [(dz, dx) for dz in dp_order for dx in reversed(range(ex_size)) if (dz, dx) != (0, 0)]
 
     def dp_at(dz):
-        return lax.rem(me_dp + dz, dp_size)
+        half = dp_size // 2
+        side = lax.rem(me_dp // half + dz // half, 2)
+        return side * half + lax.rem(me_dp + dz, half)
 
     def ex_at(dx):
         return lax.rem(me_ex + dx, ex_size)
@@ -73,7 +76,7 @@
         pltpu.make_async_copy(upstream.at[:, columns(p)], cot.at[p], token_sem.at[1, p])
         for p in range(dp_size)
     ]
-    for load in small_loads + [load_in, load_down] + tok_loads + cot_loads:
+    for load in small_loads + [load_in, load_down]:
         load.start()
 
     def page_copy(i, dz, dx, place):
@@ -128,7 +131,7 @@
         total = None
         for dz in [0] + dp_order[:-1]:
             d = dp_at(dz)
-            for dx in range(ex_size):
+            for dx in reversed(range(ex_size)):
                 if (dz, dx) != (0, 0):
                     page_copy(i, dz, dx, (d, ex_at(dx))).wait_recv()
             page = pages[d, 0:2] if i == 0 else pages[d, 2]
@@ -144,7 +147,7 @@
                 parts_out[d, 0:2] = part.reshape(2, ex_size, exp_dev, rank, piece)
             else:
                 parts_out[d, 2] = part.reshape(ex_size, exp_dev, rank, piece)
-            for dx in range(ex_size):
+            for dx in reversed(range(ex_size)):
                 if (dz, dx) != (0, 0):
                     part_copy(i, dz, dx, (me_dp, me_ex)).start()
 
@@ -154,6 +157,8 @@
     pl.semaphore_wait(barrier, len(peers) + 1)
     send_pages(0)
     load_down.wait()
+    for load in tok_loads + cot_loads:
+        load.start()
     send_pages(1)
 
     for load in small_loads[2:] + tok_loads:
@@ -232,15 +237,17 @@
 
 
 def scatter_kernel(
-    sizes, slots,
+    sizes,
     block_tenant, page_table, parts, adapted, grad_tokens, grad_weight,
     grad_in, grad_down, adapted_out, grad_tokens_out, grad_weight_out,
     tenants, table, parts_v, adapted_v, grad_tokens_v, grad_weight_v,
-    small_sem, parts_sem, enter_sem, leave_sem,
+    zeros, total_in, total_down,
+    small_sem, parts_sem, enter_sem, leave_sem, zero_sem, total_sem,
 ):
-    dp_size, ex_size, exp_dev, rank = sizes
-    local = pl.program_id(0)
-    chunk = pl.program_id(1)
+    dp_size, ex_size, exp_dev, rank, slots = sizes
+    blocks = dp_size * ex_size
+    chunk = zeros.shape[0]
+    me_ex = lax.axis_index("expert")
     loads = [
         pltpu.make_async_copy(block_tenant, tenants, small_sem.at[0]),
         pltpu.make_async_copy(page_table, table, small_sem.at[1]),
@@ -259,43 +266,88 @@
         pltpu.make_async_copy(held, target, leave_sem.at[i])
         for i, (_, held, target) in enumerate(passed)
     ]
-    step = local * pl.num_programs(1) + chunk
-
-    @pl.when(step == 0)
-    def _():
-        for load in loads + enter:
-            load.start()
-
-    grad_in[...] = jnp.zeros_like(grad_in)
-    grad_down[...] = jnp.zeros_like(grad_down)
-
-    @pl.when(step == 0)
-    def _():
-        for load in loads:
-            load.wait()
-
-    @pl.when(step == 1)
-    def _():
-        for load in enter:
-            load.wait()
-        for store in leave:
-            store.start()
-
-    expert = lax.axis_index("expert") * exp_dev + local
-    for d in range(dp_size):
-        for x in range(ex_size):
-            place = table[expert, tenants[d * ex_size + x]] - chunk * slots
-
-            @pl.when((place >= 0) & (place < slots))
+    for load in loads + enter:
+        load.start()
+
+    zeros[...] = jnp.zeros_like(zeros)
+    clears = []
+    for local in range(exp_dev):
+        for i, start in enumerate(range(0, slots, chunk)):
+            place = pl.ds(start, chunk)
+            clears.append(
+                [
+                    pltpu.make_async_copy(
+                        zeros, grad_in.at[local, place], zero_sem.at[local, i, 0]
+                    ),
+                    pltpu.make_async_copy(
+                        zeros.at[:, :rank], grad_down.at[local, place], zero_sem.at[local, i, 1]
+                    ),
+                ]
+            )
+            for clear in clears[-1]:
+                clear.start()
+
+    for load in loads:
+        load.wait()
+    tenant = [tenants[b] for b in range(blocks)]
+    leads = []
+    for b in range(blocks):
+        first = jnp.bool_(True)
+        for other in range(b):
+            first = first & (tenant[other] != tenant[b])
+        leads.append(first)
+        part = parts_v[b // ex_size, b % ex_size].astype(F32)
+        total_in[b, :, :rank] = part[0]
+        total_in[b, :, rank:] = part[1]
+        total_down[b] = part[2]
+    for b in range(blocks):
+        for later in range(b + 1, blocks):
+
+            @pl.when(leads[b] & (tenant[later] == tenant[b]))
             def _():
-                grad_in[0, place, :rank] += parts_v[d, x, 0, local].astype(F32)
-                grad_in[0, place, rank:] += parts_v[d, x, 1, local].astype(F32)
-                grad_down[0, place] += parts_v[d, x, 2, local].astype(F32)
-
-    @pl.when(step == pl.num_programs(0) * pl.num_programs(1) - 1)
-    def _():
-        for store in leave:
-            store.wait()
+                part = parts_v[later // ex_size, later % ex_size].astype(F32)
+                total_in[b, :, :rank] += part[0]
+                total_in[b, :, rank:] += part[1]
+                total_down[b] += part[2]
+
+    for load in enter:
+        load.wait()
+    for store in leave:
+        store.start()
+
+    def stores(local, b):
+        slot = table[me_ex * exp_dev + local, tenant[b]]
+        return [
+            pltpu.make_async_copy(
+                total_in.at[b, local], grad_in.at[local, slot], total_sem.at[local, b, 0]
+            ),
+            pltpu.make_async_copy(
+                total_down.at[b, local], grad_down.at[local, slot], total_sem.at[local, b, 1]
+            ),
+        ]
+
+    per_expert = slots // chunk
+    for local in range(exp_dev):
+        for pair in clears[local * per_expert : (local + 1) * per_expert]:
+            for clear in pair:
+                clear.wait()
+        for b in range(blocks):
+
+            @pl.when(leads[b])
+            def _():
+                for store in stores(local, b):
+                    store.start()
+
+    for local in range(exp_dev):
+        for b in range(blocks):
+
+            @pl.when(leads[b])
+            def _():
+                for store in stores(local, b):
+                    store.wait()
+
+    for store in leave:
+        store.wait()
 
 
 def paged(
@@ -365,10 +417,10 @@
         block_tenant, page_table, routes.T, route_weight.T,
         tokens, upstream, adapter_in, adapter_down,
     )
-    slots = 8
+    blocks = dp_size * ex_size
+    chunk = 8
     grad_in, grad_down, adapted, grad_tokens, grad_weight = pl.pallas_call(
-        functools.partial(scatter_kernel, (dp_size, ex_size, exp_dev, rank), slots),
-        grid=(exp_dev, tenants // slots),
+        functools.partial(scatter_kernel, (dp_size, ex_size, exp_dev, rank, tenants)),
         out_shape=(
             jax.ShapeDtypeStruct((exp_dev, tenants, 2 * rank, piece), F32),
             jax.ShapeDtypeStruct((exp_dev, tenants, rank, piece), F32),
@@ -377,23 +429,22 @@
             weight_shape,
         ),
         in_specs=[any_spec] * 6,
-        out_specs=(
-            pl.BlockSpec((1, slots, 2 * rank, piece), lambda i, j: (i, j, 0, 0)),
-            pl.BlockSpec((1, slots, rank, piece), lambda i, j: (i, j, 0, 0)),
-            any_spec,
-            any_spec,
-            any_spec,
-        ),
+        out_specs=(any_spec,) * 5,
         scratch_shapes=small_scratch
         + [
             pltpu.VMEM(parts_shape, BF16),
             pltpu.VMEM((tok_dev, half), BF16),
             pltpu.VMEM((tok_dev, half), BF16),
             pltpu.VMEM((top, tok_dev), F32),
+            pltpu.VMEM((chunk, 2 * rank, piece), F32),
+            pltpu.VMEM((blocks, exp_dev, 2 * rank, piece), F32),
+            pltpu.VMEM((blocks, exp_dev, rank, piece), F32),
             dma((2,)),
             dma,
             dma((3,)),
             dma((3,)),
+            dma((exp_dev, tenants // chunk, 2)),
+            dma((exp_dev, blocks, 2)),
         ],
         compiler_params=pltpu.CompilerParams(vmem_limit_bytes=60 << 20),
     )(block_tenant, page_table, parts, adapted, grad_tokens, grad_weight)
@@ -532,8 +583,9 @@
 
 def shards(*arrays):
     rank, piece = arrays[6].shape[2:]
-    whole_tiles = piece % 128 == 0 and rank % 16 == 0 and lax.axis_size("tensor") == 2
-    return paged(*arrays) if whole_tiles else routed(*arrays)
+    whole_tiles = piece % 128 == 0 and rank % 16 == 0
+    even = lax.axis_size("tensor") == 2 and lax.axis_size("dp") % 2 == 0
+    return paged(*arrays) if whole_tiles and even else routed(*arrays)
 
 
 def solution(mesh):

time: 65.7 us -> 63.6 us (0.968)
  Pallas kernels: 64.2 us -> 62.5 us
    pallas_call x1, Pallas kernels: 7.54 us -> 6.24 us  [paged(): pl.pallas_call(functools.partial(scatter_kernel, (dp_size, ex_size, exp_d...]
where the time goes in v2:
time: 63.6 us; the launch traced here: 63.2 us
  Pallas kernels  62.5 us (98%)
  between operations  0.64 us (1%)
    pallas_call x1, Pallas kernels, paged(): pl.pallas_call(functools.partial(adapter_kernel, sizes), out_shape=(rows_...  56.3 us
    pallas_call x1, Pallas kernels, paged(): pl.pallas_call(functools.partial(scatter_kernel, (dp_size, ex_size, exp_d...  6.24 us

profile of v2, /device:TPU:17, one launch (start us, length us, event | category | flops | bytes accessed | tf_op | source)
XLA Modules:
  0.0 63.2 jit_solution(3453980516507249962)
XLA Ops:
  0.6 56.3 %shard_map.119 = (bf16[128,3072]{1,0:T(8,128)(2,1)}, bf16[128,3072]{1,0:T(8,128)(2,1)}, f32[2,128]{1,0:T(2,128)}, bf16[4,2,3,2,16,768]{5,4,3,2,1,0:T(8,128)(2,1)}) custom-call(s32[8]{0:T(128)} %block_tenant.3, s32[4,32]{1,0:T(4,128)} %page_table.3, s32[2,128]{1,0:T(2,128)} %bitcast.3, f32[2,128]{1,0:T(2,128)} %bitcast.4, bf16[128,3072]{1,0:T(8,128)(2,1)} %tokens.1, ...), custom_call_target="tpu_custom_call" | custom-call | tf_op jit(solution)/shard_map/pallas_call | solution.py:373
  56.9 6.2 %shard_map.120 = (f32[2,32,32,768]{3,2,1,0:T(8,128)}, f32[2,32,16,768]{3,2,1,0:T(8,128)}, bf16[128,3072]{1,0:T(8,128)(2,1)}, bf16[128,3072]{1,0:T(8,128)(2,1)}, f32[2,128]{1,0:T(2,128)}) custom-call(s32[8]{0:T(128)} %block_tenant.3, s32[4,32]{1,0:T(4,128)} %page_table.3, bf16[4,2,3,2,16,768]{5,4,3,2,1,0:T(8,128)(2,1)} %get-tuple-element.14.parts, ...), custom_call_target="tpu_custom_call" | custom-call | tf_op jit(solution)/shard_map/pallas_call | solution.py:422
